TPU v7x, 256 devices: a whole 4x4x8 slice. The times are simulated.
256 devices in a mesh: section: 16 (over y_hi, x, core), expert: 8 (over z), dp: 2 (over y_lo).
Axes of the slice: x: 4, y: 4 (y_hi: 2, y_lo: 2; y = y_hi * 2 + y_lo), z: 8, core: 2. Of those that a mesh axis runs over, the one named last changes fastest.
Arguments:
- held_states: bfloat16 [16, 2, 512, 3584], P('section', None, ('expert', 'dp')), may hold values from -6 to 6
- entering_rows: bfloat16 [1, 2, 512, 3584], P(None, None, ('expert', 'dp')), may hold values from -6 to 6
- norm_gain: bfloat16 [16, 3584], P('section'), may hold values from 0.5 to 1.5
- router_weight: bfloat16 [16, 8, 3584], P('section'), may hold values from -0.1875 to 0.1875
- up_weight: bfloat16 [16, 8, 3584, 1024], P('section', 'expert', None, 'dp'), may hold values from -0.09375 to 0.09375
- down_weight: bfloat16 [16, 8, 1024, 3584], P('section', 'expert', 'dp'), may hold values from -0.1875 to 0.1875
- expert_routes: int32 [16, 2, 2, 512, 2], P('section', None, None, 'expert'), may hold values from 0 to 7, all different within a row; in each aligned block of 32 rows (0 to 31, 32 to 63, ..., all dimensions but the last counted through in order) at most 12 rows name the same one
- weight_cotangent: float32 [16, 2, 2, 512, 2], P('section', None, None, ('expert', 'dp')), may hold values from -6 to 6
Outputs:
- layer_out: bfloat16 [16, 2, 2, 512, 3584], P('section', None, None, ('expert', 'dp'))
- router_grads: float32 [16, 8, 3584], P('section', None, ('expert', 'dp'))
Inputs may be any that keep to these rules, and one draw needn't show every extreme that they name: `expert_routes`: each token names 2 different experts. In each aligned block of 32 tokens (the tokens of one device) no expert is named by more than 12 routes, a bound that some block reaches.
All inputs are finite; a program needn't handle non-finite values.
Results may differ from a plain program's by a relative error of at most 0.022.
Values may be sent and summed in bfloat16 or wider, within the bound.
A program may use at most 64 MiB of HBM per device.

v0:
```python
import jax
import jax.numpy as jnp
from jax import lax
from jax.sharding import PartitionSpec as P

TICKS = 2


route_scale = 2.5


def passed_along(value, axis, by):
    devices = lax.axis_size(axis)
    pairs = [(i, i + by) for i in range(devices) if 0 <= i + by < devices]
    return lax.ppermute(value, axis, pairs)


def normalize(tokens_in, gain_row):
    values = tokens_in.astype(jnp.float32)
    meansq = jnp.mean(values * values, axis=-1, keepdims=True)
    return (values * lax.rsqrt(meansq + 1e-06) * gain_row.astype(jnp.float32)).astype(jnp.bfloat16)


def gating(normed, router_rows, own_routes, expert_count):
    logits = jnp.dot(normed, router_rows.T, preferred_element_type=jnp.float32)
    route_hot = (own_routes[:, :, None] == jnp.arange(expert_count, dtype=jnp.int32)).astype(
        jnp.float32
    )
    picked = jnp.sum(logits[:, None, :] * route_hot, axis=2)
    affinity = jax.nn.sigmoid(picked)
    aff_total = jnp.sum(affinity, axis=1, keepdims=True)
    weights = route_scale * affinity / aff_total
    return (weights, affinity, aff_total, route_hot)


def router_grad(normed, affinity, aff_total, route_hot, cotangent):
    inner_sum = jnp.sum(cotangent * affinity, axis=1, keepdims=True)
    aff_grad = route_scale * (cotangent / aff_total - inner_sum / (aff_total * aff_total))
    logit_grad = aff_grad * affinity * (1.0 - affinity)
    dense_grad = jnp.sum(logit_grad[:, :, None] * route_hot, axis=1)
    return jnp.dot(
        dense_grad.T,
        normed.astype(jnp.float32),
        precision=lax.Precision.HIGHEST,
        preferred_element_type=jnp.float32,
    )


def slot_index(block_routes, expert_count):
    block_count = block_routes.shape[0]
    flat_rows = block_routes.reshape(block_count, -1)
    route_hot = (flat_rows[:, :, None] == jnp.arange(expert_count, dtype=jnp.int32)).astype(
        jnp.int32
    )
    earlier = jnp.cumsum(route_hot, axis=1) - route_hot
    return jnp.sum(earlier * route_hot, axis=2).reshape(block_routes.shape)


def expert_part(flat_rows, up_local, down_local):
    pre_act = jnp.dot(flat_rows, up_local, preferred_element_type=jnp.float32)
    hidden = jax.nn.silu(pre_act).astype(jnp.bfloat16)
    return jnp.dot(hidden, down_local, preferred_element_type=jnp.float32)


def run_layer(tokens_in, gain_row, router_rows, up_local, down_local, both_routes, cotangent):
    tok_rows = tokens_in.shape[0]
    model_width = tokens_in.shape[1]
    expert_count = router_rows.shape[0]
    route_count = both_routes.shape[-1]
    capacity = 3 * tok_rows * route_count // (2 * expert_count)
    normed = normalize(tokens_in, gain_row)
    own_routes = lax.dynamic_slice_in_dim(both_routes, lax.axis_index("dp") * tok_rows, tok_rows, 0)
    weights, affinity, aff_total, route_hot = gating(normed, router_rows, own_routes, expert_count)
    grad_part = router_grad(normed, affinity, aff_total, route_hot, cotangent)
    rows_in = normed[None]
    routes_in = own_routes[None]
    block_count = rows_in.shape[0]
    slot_rank = slot_index(routes_in, expert_count)
    block_ids = jnp.arange(block_count, dtype=jnp.int32)[:, None, None]
    slot_target = ((routes_in * block_count + block_ids) * capacity + slot_rank).reshape(-1)
    sources = jnp.repeat(rows_in.reshape(-1, model_width), route_count, axis=0)
    buffer = (
        jnp.zeros((expert_count * block_count * capacity, model_width), jnp.bfloat16)
        .at[slot_target]
        .set(sources)
    )
    buffer = buffer.reshape(expert_count, block_count, capacity, model_width)
    arrived = lax.all_to_all(buffer, "expert", split_axis=0, concat_axis=0, tiled=True)
    rows_piece = lax.all_gather(arrived, "dp", axis=1, tiled=True)
    flat_rows = rows_piece.reshape(-1, model_width)
    partial_value = expert_part(flat_rows, up_local, down_local).reshape(rows_piece.shape)
    summed = lax.psum_scatter(
        partial_value.astype(jnp.bfloat16), "dp", scatter_dimension=1, tiled=True
    )
    returned = lax.all_to_all(summed, "expert", split_axis=0, concat_axis=0, tiled=True)
    own_rank = slot_index(own_routes[None], expert_count)[0]
    own_target = (own_routes * capacity + own_rank).reshape(-1)
    gathered_back = returned.reshape(-1, model_width)[own_target].reshape(
        tok_rows, route_count, model_width
    )
    mixed = tokens_in.astype(jnp.float32) + jnp.sum(
        weights[:, :, None] * gathered_back.astype(jnp.float32), axis=1
    )
    return (mixed.astype(jnp.bfloat16), grad_part)


def per_device(
    held_states,
    entering_rows,
    norm_gain,
    router_weight,
    up_weight,
    down_weight,
    expert_routes,
    weight_cotangent,
):
    gain_row = norm_gain[0]
    router_rows = router_weight[0]
    up_local = up_weight[0, 0]
    down_local = down_weight[0, 0]
    section_now = lax.axis_index("section")
    at_first = section_now == 0
    at_last = section_now == lax.axis_size("section") - 1
    state_a = held_states[0, 0]
    state_b = held_states[0, 1]
    grad_total = jnp.zeros(router_rows.shape, jnp.float32)
    per_tick = []
    for tick_step in range(TICKS):
        mixed_a, grad_a = run_layer(
            state_a,
            gain_row,
            router_rows,
            up_local,
            down_local,
            expert_routes[0, tick_step, 0],
            weight_cotangent[0, tick_step, 0],
        )
        mixed_b, grad_b = run_layer(
            state_b,
            gain_row,
            router_rows,
            up_local,
            down_local,
            expert_routes[0, tick_step, 1],
            weight_cotangent[0, tick_step, 1],
        )
        grad_total = grad_total + grad_a + grad_b
        per_tick.append(jnp.stack([mixed_a, mixed_b], axis=0))
        if tick_step + 1 < TICKS:
            moved_a = passed_along(mixed_a, "section", 1)
            moved_b = passed_along(mixed_b, "section", -1)
            state_a = jnp.where(at_first, entering_rows[tick_step, 0], moved_a)
            state_b = jnp.where(at_last, entering_rows[tick_step, 1], moved_b)
    layer_out = jnp.stack(per_tick, axis=0)[None]
    grads = lax.psum_scatter(
        grad_total.astype(jnp.bfloat16), ("expert", "dp"), scatter_dimension=1, tiled=True
    ).astype(jnp.float32)[None]
    return (layer_out, grads)


def solution(mesh):
    placed = (
        P("section", None, ("expert", "dp"), None),
        P(None, None, ("expert", "dp"), None),
        P("section", None),
        P("section", None, None),
        P("section", "expert", None, "dp"),
        P("section", "expert", "dp", None),
        P("section", None, None, "expert", None),
        P("section", None, None, ("expert", "dp"), None),
    )
    return jax.shard_map(
        per_device,
        mesh=mesh,
        in_specs=placed,
        out_specs=(
            P("section", None, None, ("expert", "dp"), None),
            P("section", None, ("expert", "dp")),
        ),
        check_vma=False,
    )
```

profile of v0, /device:TPU:1, one launch (start us, length us, event | category | flops | bytes accessed | tf_op | source)
XLA Modules:
  0.0 510.1 jit_solution(12017062910373100331)
XLA Ops:
  13.1 1.4 scatter_custom_fusion.1
  15.7 9.0 %all-to-all-start.2 = ((bf16[8,1,12,3584]{3,2,1,0:T(8,128)(2,1)}), bf16[8,1,12,3584]{3,2,1,0:T(8,128)(2,1)S(1)}, u32[]{:S(2)}, u32[]{:S(2)}) async-start(bf16[8,1,12,3584]{3,2,1,0:T(8,128)(2,1)} %bitcast.19), calls=%async_computation.3 | async-start | bytes 1835008 | tf_op jit(solution)/shard_map/all_to_all | solution.py:88
  25.9 25.2 %all-to-all-done.2 = bf16[8,1,12,3584]{3,2,1,0:T(8,128)(2,1)S(1)} async-done(((bf16[8,1,12,3584]{3,2,1,0:T(8,128)(2,1)}), bf16[8,1,12,3584]{3,2,1,0:T(8,128)(2,1)S(1)}, u32[]{:S(2)}, u32[]{:S(2)}) %all-to-all-start.2) | async-done | bytes 688160 | tf_op jit(solution)/shard_map/all_to_all | solution.py:88
  52.4 1.4 scatter_custom_fusion
  54.0 27.9 %all_to_all.40 = bf16[8,1,12,3584]{3,2,1,0:T(8,128)(2,1)S(1)} all-to-all(bf16[8,1,12,3584]{3,2,1,0:T(8,128)(2,1)S(1)} %bitcast.232), channel_id=1, replica_groups=mesh['section'=16,'expert'=8,'dp'=2] {'expert'}, dimensions={0} | all-to-all | bytes 1376256 | tf_op jit(solution)/shard_map/all_to_all | solution.py:88
  83.3 1.8 copy.163
  85.4 3.0 multiply_convert_fusion.2
  88.5 3.2 convolution_convert_fusion.2
  91.6 1.9 copy.164
  93.6 18.6 %all-gather.5.cloned.1.call-done = bf16[8,2,12,3584]{3,0,2,1:T(8,128)(2,1)} async-done(((bf16[8,1,12,3584]{3,0,2,1:T(8,128)(2,1)}), bf16[8,2,12,3584]{3,0,2,1:T(8,128)(2,1)}) %all-gather.5.cloned.1.call-update) | async-done | bytes 1376272 | tf_op jit(solution)/shard_map/all_gather | solution.py:89
  112.2 1.8 copy.155
  114.4 3.0 multiply_convert_fusion.3
  117.4 3.2 convolution_convert_fusion.3
  120.6 1.8 copy.156
  122.4 22.3 %reduce-scatter.10.cloned.1.call-done = bf16[8,1,12,3584]{3,0,2,1:T(8,128)(2,1)} async-done(((bf16[8,2,12,3584]{3,0,2,1:T(8,128)(2,1)}), bf16[8,1,12,3584]{3,0,2,1:T(8,128)(2,1)}) %reduce-scatter.10.cloned.1.call-update) | async-done | bytes 688144 | tf_op jit(solution)/shard_map/reduce_scatter | solution.py:92
  144.8 2.3 copy.165
  147.0 7.0 %all-to-all-start.3 = ((bf16[8,1,12,3584]{3,2,1,0:T(8,128)(2,1)}), bf16[8,1,12,3584]{3,2,1,0:T(8,128)(2,1)S(1)}, u32[]{:S(2)}, u32[]{:S(2)}) async-start(bf16[8,1,12,3584]{3,2,1,0:T(8,128)(2,1)} %copy.165), calls=%async_computation.5 | async-start | bytes 1835008 | tf_op jit(solution)/shard_map/all_to_all | solution.py:95
  154.6 22.7 %reduce-scatter.8.cloned.1.call-done = bf16[8,1,12,3584]{3,0,2,1:T(8,128)(2,1)} async-done(((bf16[8,2,12,3584]{3,0,2,1:T(8,128)(2,1)}), bf16[8,1,12,3584]{3,0,2,1:T(8,128)(2,1)}) %reduce-scatter.8.cloned.1.call-update) | async-done | bytes 688144 | tf_op jit(solution)/shard_map/reduce_scatter | solution.py:92
  177.3 2.2 copy.157
  180.4 5.9 %all-to-all-start.1 = ((bf16[8,1,12,3584]{3,2,1,0:T(8,128)(2,1)}), bf16[8,1,12,3584]{3,2,1,0:T(8,128)(2,1)S(1)}, u32[]{:S(2)}, u32[]{:S(2)}) async-start(bf16[8,1,12,3584]{3,2,1,0:T(8,128)(2,1)} %copy.157), calls=%async_computation.2 | async-start | bytes 1835008 | tf_op jit(solution)/shard_map/all_to_all | solution.py:95
  192.5 20.1 %all-to-all-done.1 = bf16[8,1,12,3584]{3,2,1,0:T(8,128)(2,1)S(1)} async-done(((bf16[8,1,12,3584]{3,2,1,0:T(8,128)(2,1)}), bf16[8,1,12,3584]{3,2,1,0:T(8,128)(2,1)S(1)}, u32[]{:S(2)}, u32[]{:S(2)}) %all-to-all-start.1) | async-done | bytes 688160 | tf_op jit(solution)/shard_map/all_to_all | solution.py:95
  214.4 2.0 multiply_reduce_fusion.2
  217.7 3.6 collective-permute-start
  221.4 1.9 collective-permute-start.1
  224.3 4.4 collective-permute-done.1
  229.9 1.4 scatter_custom_fusion.2
  232.5 3.6 all-to-all-start.4
  236.9 21.8 %all-to-all-done.4 = bf16[8,1,12,3584]{3,2,1,0:T(8,128)(2,1)S(1)} async-done(((bf16[8,1,12,3584]{3,2,1,0:T(8,128)(2,1)}), bf16[8,1,12,3584]{3,2,1,0:T(8,128)(2,1)S(1)}, u32[]{:S(2)}, u32[]{:S(2)}) %all-to-all-start.4) | async-done | bytes 688160 | tf_op jit(solution)/shard_map/all_to_all | solution.py:88
  260.5 1.4 scatter_custom_fusion.3
  262.1 26.9 %all_to_all.41 = bf16[8,1,12,3584]{3,2,1,0:T(8,128)(2,1)S(1)} all-to-all(bf16[8,1,12,3584]{3,2,1,0:T(8,128)(2,1)S(1)} %bitcast.233), channel_id=1, replica_groups=mesh['section'=16,'expert'=8,'dp'=2] {'expert'}, dimensions={0} | all-to-all | bytes 1376256 | tf_op jit(solution)/shard_map/all_to_all | solution.py:88
  291.2 1.8 copy.171
  294.2 3.4 multiply_convert_fusion.1
  297.7 3.2 convolution_convert_fusion.1
  300.9 1.8 copy.172
  305.5 16.0 %all-gather.11.cloned.1.call-done = bf16[8,2,12,3584]{3,0,2,1:T(8,128)(2,1)} async-done(((bf16[8,1,12,3584]{3,0,2,1:T(8,128)(2,1)}), bf16[8,2,12,3584]{3,0,2,1:T(8,128)(2,1)}) %all-gather.11.cloned.1.call-update) | async-done | bytes 1376272 | tf_op jit(solution)/shard_map/all_gather | solution.py:89
  321.5 1.8 copy.179
  323.3 1.3 reshape.1015
  324.6 3.4 multiply_convert_fusion
  328.7 3.2 convolution_convert_fusion
  332.0 1.9 copy.180
  333.9 20.1 %reduce-scatter.12.cloned.1.call-done = bf16[8,1,12,3584]{3,0,2,1:T(8,128)(2,1)} async-done(((bf16[8,2,12,3584]{3,0,2,1:T(8,128)(2,1)}), bf16[8,1,12,3584]{3,0,2,1:T(8,128)(2,1)}) %reduce-scatter.12.cloned.1.call-update) | async-done | bytes 688144 | tf_op jit(solution)/shard_map/reduce_scatter | solution.py:92
  354.1 2.2 copy.173
  356.3 6.7 %all-to-all-start.5 = ((bf16[8,1,12,3584]{3,2,1,0:T(8,128)(2,1)}), bf16[8,1,12,3584]{3,2,1,0:T(8,128)(2,1)S(1)}, u32[]{:S(2)}, u32[]{:S(2)}) async-start(bf16[8,1,12,3584]{3,2,1,0:T(8,128)(2,1)} %copy.173), calls=%async_computation.8 | async-start | bytes 1835008 | tf_op jit(solution)/shard_map/all_to_all | solution.py:95
  363.3 58.3 %reduce-scatter.16.cloned.1.call-done = bf16[224,8]{1,0:T(8,128)(2,1)} async-done(((bf16[3584,8]{1,0:T(8,128)(2,1)}), bf16[224,8]{1,0:T(8,128)(2,1)}) %reduce-scatter.16.cloned.1.call-update) | async-done | bytes 3600
  422.5 41.4 %reduce-scatter.14.cloned.1.call-done = bf16[8,1,12,3584]{3,0,2,1:T(8,128)(2,1)} async-done(((bf16[8,2,12,3584]{3,0,2,1:T(8,128)(2,1)}), bf16[8,1,12,3584]{3,0,2,1:T(8,128)(2,1)}) %reduce-scatter.14.cloned.1.call-update) | async-done | bytes 688144 | tf_op jit(solution)/shard_map/reduce_scatter | solution.py:92
  464.0 2.2 copy.181
  466.2 6.9 %all-to-all-start.7 = ((bf16[8,1,12,3584]{3,2,1,0:T(8,128)(2,1)}), bf16[8,1,12,3584]{3,2,1,0:T(8,128)(2,1)S(1)}, u32[]{:S(2)}, u32[]{:S(2)}) async-start(bf16[8,1,12,3584]{3,2,1,0:T(8,128)(2,1)} %copy.181), calls=%async_computation.11 | async-start | bytes 1835008 | tf_op jit(solution)/shard_map/all_to_all | solution.py:95
  476.6 22.9 %all-to-all-done.7 = bf16[8,1,12,3584]{3,2,1,0:T(8,128)(2,1)S(1)} async-done(((bf16[8,1,12,3584]{3,2,1,0:T(8,128)(2,1)}), bf16[8,1,12,3584]{3,2,1,0:T(8,128)(2,1)S(1)}, u32[]{:S(2)}, u32[]{:S(2)}) %all-to-all-start.7) | async-done | bytes 688160 | tf_op jit(solution)/shard_map/all_to_all | solution.py:95
  (220 shorter events, 43.5 us)
Async XLA Ops:
  7.2 146.9 %copy-start = (bf16[1,8,3584]{2,1,0:T(8,128)(2,1)S(1)}, bf16[1,8,3584]{2,1,0:T(8,128)(2,1)}, u32[]{:S(2)}) copy-start(bf16[1,8,3584]{2,1,0:T(8,128)(2,1)} %param.11) | copy-start | bytes 172036
  12.0 13.3 %copy-start.12 = (bf16[32,3584]{1,0:T(8,128)(2,1)}, bf16[32,3584]{1,0:T(8,128)(2,1)S(1)}, u32[]{:S(2)}) copy-start(bf16[32,3584]{1,0:T(8,128)(2,1)S(1)} %get-tuple-element.28) | copy-start | bytes 688132
  15.7 35.4 %all-to-all-start.2 = ((bf16[8,1,12,3584]{3,2,1,0:T(8,128)(2,1)}), bf16[8,1,12,3584]{3,2,1,0:T(8,128)(2,1)S(1)}, u32[]{:S(2)}, u32[]{:S(2)}) async-start(bf16[8,1,12,3584]{3,2,1,0:T(8,128)(2,1)} %bitcast.19), calls=%async_computation.3 | async-start | bytes 1835008 | tf_op jit(solution)/shard_map/all_to_all | solution.py:88
  24.7 58.6 %all-gather.7.cloned.1.call-start = ((), (), s32[]{:S(2)}) async-start(), calls=%async_computation.15 | async-start | bytes 2064384 | tf_op jit(solution)/shard_map/all_gather | solution.py:89
  52.3 59.9 %all-gather.5.cloned.1.call-start = ((), (), s32[]{:S(2)}) async-start(), calls=%async_computation.13 | async-start | bytes 2064384 | tf_op jit(solution)/shard_map/all_gather | solution.py:89
  83.2 61.6 %reduce-scatter.10.cloned.1.call-start = ((), (), s32[]{:S(2)}) async-start(), calls=%async_computation.16 | async-start | bytes 2064384 | tf_op jit(solution)/shard_map/reduce_scatter | solution.py:92
  93.5 83.8 %reduce-scatter.8.cloned.1.call-start = ((), (), s32[]{:S(2)}) async-start(), calls=%async_computation.14 | async-start | bytes 2064384 | tf_op jit(solution)/shard_map/reduce_scatter | solution.py:92
  122.4 31.6 %copy-start.2 = (bf16[1,2,32,3584]{3,2,1,0:T(8,128)(2,1)S(1)}, bf16[1,2,32,3584]{3,2,1,0:T(8,128)(2,1)}, u32[]{:S(2)}) copy-start(bf16[1,2,32,3584]{3,2,1,0:T(8,128)(2,1)} %param.8) | copy-start | bytes 1376260
  147.0 33.4 %all-to-all-start.3 = ((bf16[8,1,12,3584]{3,2,1,0:T(8,128)(2,1)}), bf16[8,1,12,3584]{3,2,1,0:T(8,128)(2,1)S(1)}, u32[]{:S(2)}, u32[]{:S(2)}) async-start(bf16[8,1,12,3584]{3,2,1,0:T(8,128)(2,1)} %copy.165), calls=%async_computation.5 | async-start | bytes 1835008 | tf_op jit(solution)/shard_map/all_to_all | solution.py:95
  154.3 31.9 %copy-start.17 = (f32[32,2]{0,1:T(2,128)}, f32[32,2]{0,1:T(2,128)S(1)}, u32[]{:S(2)}) copy-start(f32[32,2]{0,1:T(2,128)S(1)} %get-tuple-element.23) | copy-start | bytes 772
  154.4 31.9 %copy-start.26 = (f32[32]{0:T(128)}, f32[32]{0:T(128)S(1)}, u32[]{:S(2)}) copy-start(f32[32]{0:T(128)S(1)} %get-tuple-element.22) | copy-start | bytes 388
  180.4 32.3 %all-to-all-start.1 = ((bf16[8,1,12,3584]{3,2,1,0:T(8,128)(2,1)}), bf16[8,1,12,3584]{3,2,1,0:T(8,128)(2,1)S(1)}, u32[]{:S(2)}, u32[]{:S(2)}) async-start(bf16[8,1,12,3584]{3,2,1,0:T(8,128)(2,1)} %copy.157), calls=%async_computation.2 | async-start | bytes 1835008 | tf_op jit(solution)/shard_map/all_to_all | solution.py:95
  187.1 1.4 copy-start.28
  213.8 2.6 copy-start.15
  216.4 6.9 %copy-start.25 = (s32[64]{0:T(128)S(1)}, s32[64]{0:T(128)}, u32[]{:S(2)}) copy-start(s32[64]{0:T(128)} %copy-done.24) | copy-start | bytes 772
  216.4 7.1 %copy-start.31 = (s32[1,1,1,32,2]{3,4,2,1,0:T(2,128)S(1)}, s32[1,1,1,32,2]{3,4,2,1,0:T(2,128)}, u32[]{:S(2)}) copy-start(s32[1,1,1,32,2]{3,4,2,1,0:T(2,128)} %get-tuple-element.48) | copy-start | bytes 772
  217.6 11.1 %copy-start.14 = (bf16[1,2,32,3584]{3,2,1,0:T(8,128)(2,1)S(1)}, bf16[1,2,32,3584]{3,2,1,0:T(8,128)(2,1)}, u32[]{:S(2)}) copy-start(bf16[1,2,32,3584]{3,2,1,0:T(8,128)(2,1)} %param.9) | copy-start | bytes 1376260
  217.7 6.6 %collective-permute-start = (bf16[32,3584]{1,0:T(8,128)(2,1)S(1)}, bf16[32,3584]{1,0:T(8,128)(2,1)S(1)}, u32[]{:S(2)}, u32[]{:S(2)}) collective-permute-start(bf16[32,3584]{1,0:T(8,128)(2,1)S(1)} %get-tuple-element.34), channel_id=1, source_target_pairs={{0,16},{16,32},{32,48},{48,64},{64,80},{80,96},{96,112},{112,128},... | collective-permute-start | bytes 688136 | tf_op jit(solution)/shard_map/ppermute | solution.py:15
  221.4 7.3 %collective-permute-start.1 = (bf16[32,3584]{1,0:T(8,128)(2,1)S(1)}, bf16[32,3584]{1,0:T(8,128)(2,1)S(1)}, u32[]{:S(2)}, u32[]{:S(2)}) collective-permute-start(bf16[32,3584]{1,0:T(8,128)(2,1)S(1)} %get-tuple-element.35), channel_id=1, source_target_pairs={{16,0},{32,16},{48,32},{64,48},{80,64},{96,80},{112,96},{128,112},... | collective-permute-start | bytes 688136 | tf_op jit(solution)/shard_map/ppermute | solution.py:15
  223.7 6.2 %copy-start.32 = (s32[64]{0:T(128)}, s32[64]{0:T(128)S(1)}, u32[]{:S(2)}) copy-start(s32[64]{0:T(128)S(1)} %fusion.105) | copy-start | bytes 772
  229.0 0.8 copy-start.8
  229.2 3.3 copy-start.3
  231.4 4.7 copy-start.19
  231.4 5.1 copy-start.30
  232.5 26.2 %all-to-all-start.4 = ((bf16[8,1,12,3584]{3,2,1,0:T(8,128)(2,1)}), bf16[8,1,12,3584]{3,2,1,0:T(8,128)(2,1)S(1)}, u32[]{:S(2)}, u32[]{:S(2)}) async-start(bf16[8,1,12,3584]{3,2,1,0:T(8,128)(2,1)} %bitcast.28), calls=%async_computation.6 | async-start | bytes 1835008 | tf_op jit(solution)/shard_map/all_to_all | solution.py:88
  236.0 55.1 %all-gather.9.cloned.1.call-start = ((), (), s32[]{:S(2)}) async-start(), calls=%async_computation.17 | async-start | bytes 2064384 | tf_op jit(solution)/shard_map/all_gather | solution.py:89
  260.0 61.5 %all-gather.11.cloned.1.call-start = ((), (), s32[]{:S(2)}) async-start(), calls=%async_computation.19 | async-start | bytes 2064384 | tf_op jit(solution)/shard_map/all_gather | solution.py:89
  260.0 2.1 copy-start.34
  289.0 2.0 copy-start.4
  290.3 63.8 %reduce-scatter.12.cloned.1.call-start = ((), (), s32[]{:S(2)}) async-start(), calls=%async_computation.18 | async-start | bytes 2064384 | tf_op jit(solution)/shard_map/reduce_scatter | solution.py:92
  300.9 2.0 copy-start.21
  300.9 2.0 copy-start.16
  300.9 2.0 copy-start.18
  300.9 2.0 copy-start.23
  300.9 2.1 copy-start.29
  300.9 2.1 copy-start.27
  300.9 2.2 copy-start.13
  300.9 2.4 copy-start.11
  302.8 1.0 copy-start.5
  302.8 118.9 %reduce-scatter.16.cloned.1.call-start = ((), (), s32[]{:S(2)}) async-start(), calls=%async_computation.21 | async-start | bytes 974848
  305.4 158.5 %reduce-scatter.14.cloned.1.call-start = ((), (), s32[]{:S(2)}) async-start(), calls=%async_computation.20 | async-start | bytes 2064384 | tf_op jit(solution)/shard_map/reduce_scatter | solution.py:92
  332.0 1.9 copy-start.33
  332.0 1.9 copy-start.35
  356.3 109.9 %all-to-all-start.5 = ((bf16[8,1,12,3584]{3,2,1,0:T(8,128)(2,1)}), bf16[8,1,12,3584]{3,2,1,0:T(8,128)(2,1)S(1)}, u32[]{:S(2)}, u32[]{:S(2)}) async-start(bf16[8,1,12,3584]{3,2,1,0:T(8,128)(2,1)} %copy.173), calls=%async_computation.8 | async-start | bytes 1835008 | tf_op jit(solution)/shard_map/all_to_all | solution.py:95
  466.2 33.3 %all-to-all-start.7 = ((bf16[8,1,12,3584]{3,2,1,0:T(8,128)(2,1)}), bf16[8,1,12,3584]{3,2,1,0:T(8,128)(2,1)S(1)}, u32[]{:S(2)}, u32[]{:S(2)}) async-start(bf16[8,1,12,3584]{3,2,1,0:T(8,128)(2,1)} %copy.181), calls=%async_computation.11 | async-start | bytes 1835008 | tf_op jit(solution)/shard_map/all_to_all | solution.py:95
  474.7 1.8 copy-start.9
  500.5 1.9 copy-start.7
  501.0 2.4 copy-start.1
  (5 other events, 3.1 us)
Sparse Core Ops, SparseCore 0:
  52.4 26.2 all-gather.6
  83.3 28.8 all-gather.4
  114.7 29.9 reduce-scatter.9
  147.3 29.9 reduce-scatter.7
  260.1 28.5 all-gather.8
  290.4 31.0 all-gather.10
  324.0 30.0 reduce-scatter.11
  357.3 64.3 reduce-scatter.15
  424.2 39.7 reduce-scatter.13
where the time goes:
time: 520 us; the launch traced here: 510 us
  waiting for transfers between devices  296 us (57%)
  local copies, waits for them, and re-layouts  57.1 us (11%)
  blocking collectives  54.9 us (11%)
  starting transfers between devices  45.5 us (9%)
  matrix products  27.1 us (5%)
  between operations  15.1 us (3%)
  other arithmetic  15 us (3%)
    reduce_scatter x4, waiting for transfers between devices, run_layer(): lax.psum_scatter(partial_value.astype(jnp.bfloat16), 'dp', scatter_dimens...  107 us
    unnamed x10, waiting for transfers between devices  58.5 us
    all_to_all x2, blocking collectives, run_layer(): lax.all_to_all(buffer, 'expert', split_axis=0, concat_axis=0, tiled=True)  54.9 us
    all_to_all x2, waiting for transfers between devices, run_layer(): lax.all_to_all(buffer, 'expert', split_axis=0, concat_axis=0, tiled=True)  47 us
    all_to_all x4, waiting for transfers between devices, run_layer(): lax.all_to_all(summed, 'expert', split_axis=0, concat_axis=0, tiled=True)  43.8 us
    all_gather x4, waiting for transfers between devices, run_layer(): rows_piece = lax.all_gather(arrived, 'dp', axis=1, tiled=True)  34.7 us
    all_to_all x4, starting transfers between devices, run_layer(): lax.all_to_all(summed, 'expert', split_axis=0, concat_axis=0, tiled=True)  26.6 us
    dot_general x4, matrix products, expert_part(): pre_act = jnp.dot(flat_rows, up_local, preferred_element_type=jnp.float32)  12.8 us
  transfers between devices with their start and end apart: 17, of which 14 were waited for; matrix products, arithmetic and copies ran while one was open for 15% of the time, Pallas kernels for 0%

commit v1 on v0

v1 whole, which is shorter than its diff:
```python
import functools

import jax
import jax.numpy as jnp
from jax import lax
from jax.experimental import pallas as pl
from jax.experimental.pallas import tpu as pltpu
from jax.sharding import PartitionSpec as P

TICKS = 2
UNITS = 4
D = 3584
TOK = 32
NE = 8
HALF = D // 2
QUART = D // 4
PACK = HALF + QUART
ROWS = NE * 16
PART = D // 16
SCALE = 2.5
MESH = pl.DeviceIdType.MESH
F32 = jnp.float32
BF16 = jnp.bfloat16
RING = (1, 7, 2, 6, 3, 5, 4)


def dot(a, b):
    return jnp.dot(a, b, preferred_element_type=F32)


def split_two(value):
    high = value.astype(BF16)
    return high, (value - high.astype(F32)).astype(BF16)


def kernel(
    held,
    entering,
    gain,
    router,
    up_hbm,
    down_hbm,
    routes,
    cot,
    out_hbm,
    grads,
    states,
    normed,
    up,
    down,
    packed,
    gath,
    part,
    yret,
    summed,
    back,
    outs,
    place,
    place_a,
    place_b,
    mix_a,
    mix_b,
    dense,
    gfull,
    gsend,
    grecv,
    gsum,
    gall,
    in_sem,
    out_sem,
    zs,
    zr,
    ys,
    yr,
    ss,
    sr,
    rs,
    rr,
    hs,
    hr,
    gs,
    gr,
):
    sec = lax.axis_index("section")
    me = lax.axis_index("expert")
    dp = lax.axis_index("dp")
    sections = lax.axis_size("section")

    def ring(offset):
        return lax.rem(me + offset + NE, NE)

    def block(index):
        return pl.ds(pl.multiple_of(index * 16, 16), 16)

    def other(index):
        return pl.ds(pl.multiple_of(index * 16 + ROWS, 16), 16)

    barrier = pltpu.get_barrier_semaphore()
    for offset in RING:
        pl.semaphore_signal(barrier, inc=1, device_id={"expert": ring(offset)}, device_id_type=MESH)
    pl.semaphore_signal(barrier, inc=1, device_id={"dp": 1 - dp}, device_id_type=MESH)

    @pl.when(sec > 0)
    def _():
        pl.semaphore_signal(barrier, inc=1, device_id={"section": sec - 1}, device_id_type=MESH)

    @pl.when(sec < sections - 1)
    def _():
        pl.semaphore_signal(barrier, inc=1, device_id={"section": sec + 1}, device_id_type=MESH)

    loads = [
        pltpu.make_async_copy(held.at[0, 0], states.at[0], in_sem.at[0]),
        pltpu.make_async_copy(held.at[0, 1], states.at[1], in_sem.at[1]),
        pltpu.make_async_copy(up_hbm.at[0, 0], up, in_sem.at[2]),
        pltpu.make_async_copy(down_hbm.at[0, 0], down, in_sem.at[3]),
    ]
    for load in loads:
        load.start()
    enter_up = pltpu.make_async_copy(entering.at[0, 0], states.at[2], in_sem.at[4])
    enter_down = pltpu.make_async_copy(entering.at[0, 1], states.at[3], in_sem.at[5])

    @pl.when(sec == 0)
    def _():
        enter_up.start()

    @pl.when(sec == sections - 1)
    def _():
        enter_down.start()

    def z_copy(u, i):
        to = ring(RING[i])
        return pltpu.make_async_remote_copy(
            src_ref=packed.at[u, block(to)],
            dst_ref=gath.at[u, block(me)],
            send_sem=zs.at[u, i],
            recv_sem=zr.at[u, i],
            device_id={"expert": to},
            device_id_type=MESH,
        )

    def origin(i):
        return me if i == 7 else ring(-RING[i])

    def y_copy(u, i):
        src = packed if i == 7 else gath
        return pltpu.make_async_remote_copy(
            src_ref=src.at[u, block(origin(i))],
            dst_ref=gath.at[u, other(origin(i))],
            send_sem=ys.at[u, i],
            recv_sem=yr.at[u, i],
            device_id={"dp": 1 - dp},
            device_id_type=MESH,
        )

    def target(i):
        return me if i == 7 else ring(RING[i])

    def s_copy(u, i):
        return pltpu.make_async_remote_copy(
            src_ref=part.at[u, other(target(i))],
            dst_ref=yret.at[u, block(target(i))],
            send_sem=ss.at[u, i],
            recv_sem=sr.at[u, i],
            device_id={"dp": 1 - dp},
            device_id_type=MESH,
        )

    def r_copy(u, i):
        to = ring(RING[i])
        return pltpu.make_async_remote_copy(
            src_ref=summed.at[u, block(to)],
            dst_ref=back.at[u, block(me)],
            send_sem=rs.at[u, i],
            recv_sem=rr.at[u, i],
            device_id={"expert": to},
            device_id_type=MESH,
        )

    def h_copy(d):
        return pltpu.make_async_remote_copy(
            src_ref=outs.at[d],
            dst_ref=states.at[2 + d],
            send_sem=hs.at[d],
            recv_sem=hr.at[d],
            device_id={"section": sec + 1 if d == 0 else sec - 1},
            device_id_type=MESH,
        )

    def g_copy(i):
        if i == 7:
            return pltpu.make_async_remote_copy(
                src_ref=gsend.at[1 - dp],
                dst_ref=grecv,
                send_sem=gs.at[7],
                recv_sem=gr.at[7],
                device_id={"dp": 1 - dp},
                device_id_type=MESH,
            )
        to = ring(RING[i])
        return pltpu.make_async_remote_copy(
            src_ref=gsum.at[to],
            dst_ref=gall.at[me],
            send_sem=gs.at[i],
            recv_sem=gr.at[i],
            device_id={"expert": to},
            device_id_type=MESH,
        )

    def rows_of(u):
        return slice(u * TOK, (u + 1) * TOK)

    def own_routes(u):
        return routes[0, u // 2, u % 2, pl.ds(pl.multiple_of(dp * TOK, TOK), TOK), :]

    def slots(u):
        chosen = own_routes(u)
        lane = lax.broadcasted_iota(jnp.int32, (TOK, ROWS), 1)
        expert, row = lane // 16, lane % 16
        hit = (chosen[:, 0:1] == expert) | (chosen[:, 1:2] == expert)
        earlier = lax.broadcasted_iota(jnp.int32, (TOK, TOK), 0) > lax.broadcasted_iota(
            jnp.int32, (TOK, TOK), 1
        )
        rank = dot(earlier.astype(F32).astype(BF16), hit.astype(F32).astype(BF16)).astype(jnp.int32)
        first = hit & (rank == row % 8)
        last = hit & (rank == 8 + row % 4)
        pa = jnp.concatenate([(first & (row // 8 == h)).astype(F32) for h in range(2)], axis=0)
        pb = jnp.concatenate([(last & (row // 4 == q)).astype(F32) for q in range(4)], axis=0)
        place[u, 0:64] = pa
        place[u, 64:192] = pb
        place_a[u] = pa.T.astype(BF16)
        place_b[u] = pb.T.astype(BF16)

    def norm(u):
        values = states[u].astype(F32)
        meansq = jnp.mean(values * values, axis=-1, keepdims=True)
        normed[rows_of(u)] = (
            values * lax.rsqrt(meansq + 1e-06) * gain[...].astype(F32)
        ).astype(BF16)

    def pack(u):
        own = normed[rows_of(u)]
        halves = jnp.concatenate([own[:, :HALF], own[:, HALF:]], axis=0)
        packed[u, :, 0:HALF] = dot(place_a[u], halves).astype(BF16)
        quarters = jnp.concatenate([own[:, q * QUART : (q + 1) * QUART] for q in range(4)], axis=0)
        packed[u, :, HALF:] = dot(place_b[u], quarters).astype(BF16)

    def dispatch(u):
        for i in range(7):
            z_copy(u, i).start()
        y_copy(u, 7).start()
        gath[u, block(me)] = packed[u, block(me)]

    def forward(u, i):
        z_copy(u, i).wait_recv()
        y_copy(u, i).start()

    def gate(u):
        chosen = own_routes(u)
        cotangent = cot[0, u // 2, u % 2]
        logits = lax.dot_general(
            normed[rows_of(u)], router[0], (((1,), (1,)), ((), ())), preferred_element_type=F32
        )
        lane = lax.broadcasted_iota(jnp.int32, (TOK, NE), 1)
        hit0, hit1 = chosen[:, 0:1] == lane, chosen[:, 1:2] == lane
        affinity = jnp.where(hit0 | hit1, jax.nn.sigmoid(logits), 0.0)
        total = jnp.sum(affinity, axis=1, keepdims=True)
        weights = SCALE * affinity / total
        cots = jnp.where(hit0, cotangent[:, 0:1], 0.0) + jnp.where(hit1, cotangent[:, 1:2], 0.0)
        inner = jnp.sum(cots * affinity, axis=1, keepdims=True)
        slope = SCALE * (cots / total - inner / (total * total))
        dense[rows_of(u)] = slope * affinity * (1.0 - affinity)
        expert = lax.broadcasted_iota(jnp.int32, (TOK, ROWS), 1) // 16
        spread = jnp.zeros((TOK, ROWS), F32)
        for e in range(NE):
            spread = jnp.where(expert == e, weights[:, e : e + 1], spread)
        high, low = split_two(spread)
        high, low = high.astype(F32), low.astype(F32)
        for h in range(6):
            hot = place[u, h * TOK : (h + 1) * TOK]
            both = jnp.concatenate([hot * high, hot * low], axis=0).astype(BF16)
            if h < 2:
                mix_a[u, h * 64 : (h + 1) * 64] = both
            else:
                mix_b[u, (h - 2) * 64 : (h - 1) * 64] = both

    def hidden(u):
        first = gath[u, :, 0:HALF]
        left = dot(first, up[0:HALF]).reshape(16, 2, 8, 512)
        right = dot(first, up[HALF:]).reshape(16, 2, 8, 512)
        pre_a = (left[:, 0] + right[:, 1]).reshape(128, 512)
        last = gath[u, :, HALF:]
        upper = lax.broadcasted_iota(jnp.int32, (16, 8, 512), 1) < 4
        quart = [
            dot(last, up[g * QUART : (g + 1) * QUART]).reshape(16, 2, 8, 512)[:, g // 2]
            for g in range(4)
        ]
        halves = jnp.where(upper, quart[0] + quart[2], quart[1] + quart[3])
        pre_b = (halves + pltpu.roll(halves, 4, 1)).reshape(128, 512)
        act_a = (pre_a * jax.nn.sigmoid(pre_a)).astype(BF16)
        act_b = (pre_b * jax.nn.sigmoid(pre_b)).astype(BF16)
        return act_a, act_b

    def project(u, act_a, act_b, side):
        acts = jnp.concatenate(
            [act_a[side * 64 : side * 64 + 64], act_b[side * 64 : side * 64 + 64]], axis=0
        )
        left = dot(acts, down[:, 0:HALF])
        right = dot(acts, down[:, HALF:])
        rows = slice(side * ROWS, side * ROWS + ROWS)
        first = jnp.concatenate(
            [left[0:64].reshape(8, 8, HALF), right[0:64].reshape(8, 8, HALF)], axis=1
        )
        part[u, rows, 0:HALF] = first.reshape(ROWS, HALF).astype(BF16)
        left_b, right_b = left[64:].reshape(8, 8, HALF), right[64:].reshape(8, 8, HALF)
        upper = lax.broadcasted_iota(jnp.int32, (8, 8, QUART), 1) < 4
        last = jnp.concatenate(
            [
                jnp.where(upper, left_b[:, :, :QUART], left_b[:, :, QUART:]),
                jnp.where(upper, right_b[:, :, :QUART], right_b[:, :, QUART:]),
            ],
            axis=1,
        )
        part[u, rows, HALF:] = last.reshape(ROWS, QUART).astype(BF16)

    def compute(u, between=()):
        between = list(between)

        def run(count):
            for _ in range(min(count, len(between))):
                between.pop(0)()

        for i in range(8):
            y_copy(u, i).wait_recv()
        act_a, act_b = hidden(u)
        run(3)
        project(u, act_a, act_b, 1)
        for i in range(8):
            s_copy(u, i).start()
        run(2)
        project(u, act_a, act_b, 0)
        run(len(between))

    def give_back(u, i):
        s_copy(u, i).wait_recv()
        rows = block(target(i))
        value = (part[u, rows].astype(F32) + yret[u, rows].astype(F32)).astype(BF16)
        if i == 7:
            back[u, rows] = value
        else:
            summed[u, rows] = value
            r_copy(u, i).start()

    def combine(u):
        for i in range(7):
            r_copy(u, i).wait_recv()
        first = dot(mix_a[u], back[u, :, 0:HALF])
        last = dot(mix_b[u], back[u, :, HALF:])
        for q in range(4):
            h, c = q // 2, (q % 2) * QUART
            mixed = (
                states[u, :, q * QUART : (q + 1) * QUART].astype(F32)
                + first[h * 64 : h * 64 + 32, c : c + QUART]
                + first[h * 64 + 32 : h * 64 + 64, c : c + QUART]
                + last[q * 64 : q * 64 + 32]
                + last[q * 64 + 32 : q * 64 + 64]
            )
            outs[u, :, q * QUART : (q + 1) * QUART] = mixed.astype(BF16)
        out_copy(u).start()

    def out_copy(u):
        return pltpu.make_async_copy(outs.at[u], out_hbm.at[0, u // 2, u % 2], out_sem.at[u])

    def sends(d):
        return sec < sections - 1 if d == 0 else sec > 0

    def takes(d):
        return sec > 0 if d == 0 else sec < sections - 1

    def shift(d):
        @pl.when(sends(d))
        def _():
            h_copy(d).start()

    def arrive(d):
        @pl.when(takes(d))
        def _():
            h_copy(d).wait_recv()

        @pl.when(jnp.logical_not(takes(d)))
        def _():
            (enter_up if d == 0 else enter_down).wait()

    def grad_local():
        turned = dense[...].T
        high, rest = split_two(turned)
        mid, low = split_two(turned - high.astype(F32))
        stacked = jnp.concatenate(
            [high.astype(F32), mid.astype(F32), low.astype(F32), jnp.zeros((8, 4 * TOK), F32)], axis=0
        ).astype(BF16)
        terms = dot(stacked, normed[...])
        gfull[:, 0:D] = terms[0:8] + terms[8:16] + terms[16:24]
        gfull[:, D:] = jnp.zeros((8, 128), F32)
        for p in range(16):
            piece = gfull[:, p * PART : p * PART + 256]
            gsend[p % 2, p // 2] = jnp.concatenate(
                [piece, jnp.zeros((8, 256), F32)], axis=0
            ).astype(BF16)
        g_copy(7).start()

    def grad_share():
        g_copy(7).wait_recv()
        gsum[...] = (gsend[dp].astype(F32) + grecv[...].astype(F32)).astype(BF16)
        for i in range(7):
            g_copy(i).start()
        gall[me] = gsum[me]

    def grad_total():
        for i in range(7):
            g_copy(i).wait_recv()
        grads[0] = jnp.sum(gall[...].astype(F32), axis=0)[0:8, 0:PART]

    fwd = [[functools.partial(forward, u, i) for i in range(7)] for u in range(UNITS)]
    ret = [[functools.partial(give_back, u, i) for i in range(8)] for u in range(UNITS)]

    slots(0)
    loads[0].wait()
    norm(0)
    pack(0)
    greeted = 8 + (sec > 0).astype(jnp.int32) + (sec < sections - 1).astype(jnp.int32)
    pl.semaphore_wait(barrier, greeted)
    dispatch(0)
    slots(1)
    loads[1].wait()
    norm(1)
    pack(1)
    dispatch(1)
    gate(0)
    gate(1)
    slots(2)
    slots(3)
    for step in fwd[0]:
        step()
    loads[2].wait()
    loads[3].wait()
    for tick in range(TICKS):
        a, b = 2 * tick, 2 * tick + 1
        compute(a, fwd[b])
        compute(b, ret[a][:5])
        for step in ret[a][5:]:
            step()
        for step in ret[b][:2]:
            step()
        combine(a)
        if tick + 1 < TICKS:
            shift(0)
        for step in ret[b][2:]:
            step()
        if tick + 1 < TICKS:
            arrive(0)
            norm(a + 2)
            pack(a + 2)
            dispatch(a + 2)
            gate(a + 2)
        combine(b)
        if tick + 1 < TICKS:
            shift(1)
            arrive(1)
            norm(b + 2)
            pack(b + 2)
            dispatch(b + 2)
            gate(b + 2)
            grad_local()
            for step in fwd[a + 2]:
                step()
            grad_share()
    grad_total()

    for u in range(UNITS):
        for i in range(7):
            z_copy(u, i).wait_send()
            r_copy(u, i).wait_send()
        for i in range(8):
            y_copy(u, i).wait_send()
            s_copy(u, i).wait_send()
        out_copy(u).wait()
    for i in range(8):
        g_copy(i).wait_send()
    for d in range(2):

        @pl.when(sends(d))
        def _():
            h_copy(d).wait_send()


def per_device(held, entering, gain, router, up, down, routes, cot):
    width = up.shape[-1]
    hbm = pl.BlockSpec(memory_space=pl.ANY)
    vmem = pl.BlockSpec(memory_space=pltpu.VMEM)
    dma = pltpu.SemaphoreType.DMA
    return pl.pallas_call(
        kernel,
        out_shape=(
            jax.ShapeDtypeStruct((1, TICKS, 2, TOK, D), BF16),
            jax.ShapeDtypeStruct((1, NE, PART), F32),
        ),
        in_specs=[hbm, hbm, vmem, vmem, hbm, hbm, vmem, vmem],
        out_specs=(hbm, vmem),
        scratch_shapes=[
            pltpu.VMEM((UNITS, TOK, D), BF16),
            pltpu.VMEM((UNITS * TOK, D), BF16),
            pltpu.VMEM((D, width), BF16),
            pltpu.VMEM((width, D), BF16),
            pltpu.VMEM((UNITS, ROWS, PACK), BF16),
            pltpu.VMEM((UNITS, 2 * ROWS, PACK), BF16),
            pltpu.VMEM((UNITS, 2 * ROWS, PACK), BF16),
            pltpu.VMEM((UNITS, ROWS, PACK), BF16),
            pltpu.VMEM((UNITS, ROWS, PACK), BF16),
            pltpu.VMEM((UNITS, ROWS, PACK), BF16),
            pltpu.VMEM((UNITS, TOK, D), BF16),
            pltpu.VMEM((UNITS, 192, ROWS), F32),
            pltpu.VMEM((UNITS, ROWS, 64), BF16),
            pltpu.VMEM((UNITS, ROWS, ROWS), BF16),
            pltpu.VMEM((UNITS, 128, ROWS), BF16),
            pltpu.VMEM((UNITS, 256, ROWS), BF16),
            pltpu.VMEM((UNITS * TOK, NE), F32),
            pltpu.VMEM((NE, D + 128), F32),
            pltpu.VMEM((2, NE, 16, 256), BF16),
            pltpu.VMEM((NE, 16, 256), BF16),
            pltpu.VMEM((NE, 16, 256), BF16),
            pltpu.VMEM((NE, 16, 256), BF16),
            dma((6,)),
            dma((UNITS,)),
            dma((UNITS, 7)),
            dma((UNITS, 7)),
            dma((UNITS, 8)),
            dma((UNITS, 8)),
            dma((UNITS, 8)),
            dma((UNITS, 8)),
            dma((UNITS, 7)),
            dma((UNITS, 7)),
            dma((2,)),
            dma((2,)),
            dma((8,)),
            dma((8,)),
        ],
        compiler_params=pltpu.CompilerParams(
            collective_id=0, has_side_effects=True, vmem_limit_bytes=56 << 20
        ),
        cost_estimate=pl.CostEstimate(
            flops=12_000_000_000, bytes_accessed=12_000_000, transcendentals=1_000_000
        ),
    )(held, entering, gain, router, up, down, routes, cot)


def solution(mesh):
    placed = (
        P("section", None, ("expert", "dp"), None),
        P(None, None, ("expert", "dp"), None),
        P("section", None),
        P("section", None, None),
        P("section", "expert", None, "dp"),
        P("section", "expert", "dp", None),
        P("section", None, None, "expert", None),
        P("section", None, None, ("expert", "dp"), None),
    )
    return jax.shard_map(
        per_device,
        mesh=mesh,
        in_specs=placed,
        out_specs=(
            P("section", None, None, ("expert", "dp"), None),
            P("section", None, ("expert", "dp")),
        ),
        check_vma=False,
    )
```

time: 520 us -> 197 us (0.38)
  the two profiles are of different devices: /device:TPU:1 before, /device:TPU:15 now
where the time goes in v1:
time: 197 us
  Pallas kernels  190 us (96%)
  local copies, waits for them, and re-layouts  6.33 us (3%)
    pallas_call x1, Pallas kernels, per_device(): pl.pallas_call(kernel, out_shape=(jax.ShapeDtypeStruct((1, TICKS, 2, TOK,...  190 us
    unnamed x4, local copies, waits for them, and re-layouts  6.33 us

profile of v1, /device:TPU:15, one launch (start us, length us, event | category | flops | bytes accessed | tf_op | source)
XLA Modules:
  0.0 197.3 jit_solution(12366613593515848591)
XLA Ops:
  0.6 1.4 copy.11.cot
  2.0 1.5 copy.10.routes
  3.5 190.3 %shard_map.95 = (bf16[1,2,2,32,3584]{4,3,2,1,0:T(8,128)(2,1)}, f32[1,8,224]{2,1,0:T(8,128)}) custom-call(bf16[1,2,32,3584]{3,2,1,0:T(8,128)(2,1)} %held.1, bf16[1,2,32,3584]{3,2,1,0:T(8,128)(2,1)} %entering.1, bf16[1,3584]{1,0:T(2,128)(2,1)} %gain.1, bf16[1,8,3584]{2,1,0:T(8,128)(2,1)} %router.1, bf16[1,1,3584,512]{3,2,1,0:T(8,128)(2,1)} %up_hbm.1, ...), custom_call_target="tpu_custom_call" | custom-call | flops 12000000000 | bytes 12000000 | tf_op jit(solution)/shard_map/pallas_call | solution.py:500
  193.8 2.2 %copy.14 = bf16[1,2,2,32,3584]{4,3,2,1,0:T(8,128)(2,1)} copy(bf16[1,2,2,32,3584]{4,3,2,1,0:T(8,128)(2,1)} %get-tuple-element.4) | data formatting | bytes 1835008
  196.0 1.3 copy.15

commit v2 on v1

--- a/solution.py
+++ b/solution.py
@@ -22,6 +22,7 @@
 F32 = jnp.float32
 BF16 = jnp.bfloat16
 RING = (1, 7, 2, 6, 3, 5, 4)
+BACK = (4, 3, 5, 2, 6, 1, 7)
 
 
 def dot(a, b):
@@ -60,6 +61,8 @@
     place_b,
     mix_a,
     mix_b,
+    route_rows,
+    cot_rows,
     dense,
     gfull,
     gsend,
@@ -153,7 +156,7 @@
         )
 
     def target(i):
-        return me if i == 7 else ring(RING[i])
+        return me if i == 7 else ring(BACK[i])
 
     def s_copy(u, i):
         return pltpu.make_async_remote_copy(
@@ -166,7 +169,7 @@
         )
 
     def r_copy(u, i):
-        to = ring(RING[i])
+        to = ring(BACK[i])
         return pltpu.make_async_remote_copy(
             src_ref=summed.at[u, block(to)],
             dst_ref=back.at[u, block(me)],
@@ -209,8 +212,14 @@
     def rows_of(u):
         return slice(u * TOK, (u + 1) * TOK)
 
+    def turn():
+        pairs = [(t, d) for t in range(TICKS) for d in range(2)]
+        named = jnp.concatenate([routes[0, t, d] for t, d in pairs], axis=0)
+        route_rows[...] = named.astype(F32).T.astype(jnp.int32)
+        cot_rows[...] = jnp.concatenate([cot[0, t, d] for t, d in pairs], axis=0).T
+
     def own_routes(u):
-        return routes[0, u // 2, u % 2, pl.ds(pl.multiple_of(dp * TOK, TOK), TOK), :]
+        return route_rows[pl.ds(pl.multiple_of(dp * TOK, TOK), TOK), 2 * u : 2 * u + 2]
 
     def slots(u):
         chosen = own_routes(u)
@@ -256,7 +265,7 @@
 
     def gate(u):
         chosen = own_routes(u)
-        cotangent = cot[0, u // 2, u % 2]
+        cotangent = cot_rows[:, 2 * u : 2 * u + 2]
         logits = lax.dot_general(
             normed[rows_of(u)], router[0], (((1,), (1,)), ((), ())), preferred_element_type=F32
         )
@@ -419,61 +428,163 @@
             g_copy(i).wait_recv()
         grads[0] = jnp.sum(gall[...].astype(F32), axis=0)[0:8, 0:PART]
 
-    fwd = [[functools.partial(forward, u, i) for i in range(7)] for u in range(UNITS)]
-    ret = [[functools.partial(give_back, u, i) for i in range(8)] for u in range(UNITS)]
-
+    turn()
     slots(0)
     loads[0].wait()
     norm(0)
     pack(0)
-    greeted = 8 + (sec > 0).astype(jnp.int32) + (sec < sections - 1).astype(jnp.int32)
-    pl.semaphore_wait(barrier, greeted)
-    dispatch(0)
+    pl.semaphore_wait(barrier, 8 + (sec > 0).astype(jnp.int32) + (sec < sections - 1).astype(jnp.int32))
+    z_copy(0, 0).start()
+    z_copy(0, 1).start()
+    z_copy(0, 2).start()
+    z_copy(0, 3).start()
+    z_copy(0, 4).start()
+    z_copy(0, 5).start()
+    z_copy(0, 6).start()
+    y_copy(0, 7).start()
+    gath[0, block(me)] = packed[0, block(me)]
     slots(1)
     loads[1].wait()
     norm(1)
     pack(1)
-    dispatch(1)
+    z_copy(1, 0).start()
+    z_copy(1, 1).start()
+    z_copy(1, 2).start()
+    z_copy(1, 3).start()
+    z_copy(1, 4).start()
+    z_copy(1, 5).start()
+    z_copy(1, 6).start()
+    y_copy(1, 7).start()
+    gath[1, block(me)] = packed[1, block(me)]
     gate(0)
     gate(1)
+    forward(0, 0)
+    forward(0, 1)
+    forward(0, 2)
+    forward(0, 3)
+    forward(0, 4)
+    forward(0, 5)
+    forward(0, 6)
+    loads[2].wait()
+    loads[3].wait()
     slots(2)
     slots(3)
-    for step in fwd[0]:
-        step()
-    loads[2].wait()
-    loads[3].wait()
-    for tick in range(TICKS):
-        a, b = 2 * tick, 2 * tick + 1
-        compute(a, fwd[b])
-        compute(b, ret[a][:5])
-        for step in ret[a][5:]:
-            step()
-        for step in ret[b][:2]:
-            step()
-        combine(a)
-        if tick + 1 < TICKS:
-            shift(0)
-        for step in ret[b][2:]:
-            step()
-        if tick + 1 < TICKS:
-            arrive(0)
-            norm(a + 2)
-            pack(a + 2)
-            dispatch(a + 2)
-            gate(a + 2)
-        combine(b)
-        if tick + 1 < TICKS:
-            shift(1)
-            arrive(1)
-            norm(b + 2)
-            pack(b + 2)
-            dispatch(b + 2)
-            gate(b + 2)
-            grad_local()
-            for step in fwd[a + 2]:
-                step()
-            grad_share()
+    forward(1, 0)
+    forward(1, 1)
+    for i in range(8):
+        y_copy(0, i).wait_recv()
+    hid0 = hidden(0)
+    project(0, *hid0, 1)
+    for i in range(8):
+        s_copy(0, i).start()
+    forward(1, 2)
+    forward(1, 3)
+    project(0, *hid0, 0)
+    forward(1, 4)
+    give_back(0, 0)
+    forward(1, 5)
+    give_back(0, 1)
+    forward(1, 6)
+    give_back(0, 2)
+    give_back(0, 3)
+    for i in range(8):
+        y_copy(1, i).wait_recv()
+    hid1 = hidden(1)
+    project(1, *hid1, 1)
+    for i in range(8):
+        s_copy(1, i).start()
+    give_back(0, 4)
+    give_back(0, 5)
+    project(1, *hid1, 0)
+    give_back(0, 6)
+    give_back(0, 7)
+    give_back(1, 0)
+    give_back(1, 1)
+    combine(0)
+    shift(0)
+    give_back(1, 2)
+    give_back(1, 3)
+    arrive(0)
+    norm(2)
+    pack(2)
+    z_copy(2, 0).start()
+    z_copy(2, 1).start()
+    z_copy(2, 2).start()
+    z_copy(2, 3).start()
+    z_copy(2, 4).start()
+    z_copy(2, 5).start()
+    z_copy(2, 6).start()
+    y_copy(2, 7).start()
+    gath[2, block(me)] = packed[2, block(me)]
+    gate(2)
+    give_back(1, 4)
+    forward(2, 0)
+    give_back(1, 5)
+    forward(2, 1)
+    give_back(1, 6)
+    forward(2, 2)
+    give_back(1, 7)
+    forward(2, 3)
+    combine(1)
+    shift(1)
+    forward(2, 4)
+    arrive(1)
+    norm(3)
+    pack(3)
+    z_copy(3, 0).start()
+    z_copy(3, 1).start()
+    z_copy(3, 2).start()
+    z_copy(3, 3).start()
+    z_copy(3, 4).start()
+    z_copy(3, 5).start()
+    z_copy(3, 6).start()
+    y_copy(3, 7).start()
+    gath[3, block(me)] = packed[3, block(me)]
+    forward(2, 5)
+    forward(2, 6)
+    gate(3)
+    grad_local()
+    grad_share()
+    forward(3, 0)
+    forward(3, 1)
+    for i in range(8):
+        y_copy(2, i).wait_recv()
+    hid2 = hidden(2)
+    project(2, *hid2, 1)
+    for i in range(8):
+        s_copy(2, i).start()
+    forward(3, 2)
+    forward(3, 3)
+    project(2, *hid2, 0)
+    forward(3, 4)
+    give_back(2, 0)
+    forward(3, 5)
+    give_back(2, 1)
+    forward(3, 6)
+    give_back(2, 2)
+    give_back(2, 3)
+    for i in range(8):
+        y_copy(3, i).wait_recv()
+    hid3 = hidden(3)
+    project(3, *hid3, 1)
+    for i in range(8):
+        s_copy(3, i).start()
+    give_back(2, 4)
+    give_back(2, 5)
+    project(3, *hid3, 0)
+    give_back(2, 6)
+    give_back(2, 7)
+    give_back(3, 0)
+    give_back(3, 1)
+    combine(2)
+    give_back(3, 2)
+    give_back(3, 3)
+    give_back(3, 4)
+    give_back(3, 5)
+    give_back(3, 6)
+    give_back(3, 7)
     grad_total()
+    combine(3)
 
     for u in range(UNITS):
         for i in range(7):
@@ -522,6 +633,8 @@
             pltpu.VMEM((UNITS, ROWS, ROWS), BF16),
             pltpu.VMEM((UNITS, 128, ROWS), BF16),
             pltpu.VMEM((UNITS, 256, ROWS), BF16),
+            pltpu.VMEM((2 * TOK, 2 * UNITS), jnp.int32),
+            pltpu.VMEM((TOK, 2 * UNITS), F32),
             pltpu.VMEM((UNITS * TOK, NE), F32),
             pltpu.VMEM((NE, D + 128), F32),
             pltpu.VMEM((2, NE, 16, 256), BF16),
@@ -549,7 +662,7 @@
         cost_estimate=pl.CostEstimate(
             flops=12_000_000_000, bytes_accessed=12_000_000, transcendentals=1_000_000
         ),
-    )(held, entering, gain, router, up, down, routes, cot)
+    )(held, entering, gain, router, up, down, jnp.swapaxes(routes, 3, 4), jnp.swapaxes(cot, 3, 4))
 
 
 def solution(mesh):

time: 197 us -> 173 us (0.88); the launches traced: 197 us -> 171 us
  Pallas kernels: 190 us -> 167 us
  local copies, waits for them, and re-layouts: 6.33 us -> 3.46 us
    pallas_call x1, Pallas kernels: 190 us -> 167 us  [per_device(): pl.pallas_call(kernel, out_shape=(jax.ShapeDtypeStruct((1, TICKS, 2, TOK,...]
    unnamed x4 -> x2, local copies, waits for them, and re-layouts: 6.33 us -> 3.46 us
where the time goes in v2:
time: 173 us; the launch traced here: 171 us
  Pallas kernels  167 us (97%)
  local copies, waits for them, and re-layouts  3.46 us (2%)
    pallas_call x1, Pallas kernels, per_device(): pl.pallas_call(kernel, out_shape=(jax.ShapeDtypeStruct((1, TICKS, 2, TOK,...  167 us

profile of v2, /device:TPU:15, one launch (start us, length us, event | category | flops | bytes accessed | tf_op | source)
XLA Modules:
  0.0 170.9 jit_solution(3336188247684386423)
XLA Ops:
  0.6 166.8 %shard_map.95 = (bf16[1,2,2,32,3584]{4,3,2,1,0:T(8,128)(2,1)}, f32[1,8,224]{2,1,0:T(8,128)}) custom-call(bf16[1,2,32,3584]{3,2,1,0:T(8,128)(2,1)} %held.1, bf16[1,2,32,3584]{3,2,1,0:T(8,128)(2,1)} %entering.1, bf16[1,3584]{1,0:T(2,128)(2,1)} %gain.1, bf16[1,8,3584]{2,1,0:T(8,128)(2,1)} %router.1, bf16[1,1,3584,512]{3,2,1,0:T(8,128)(2,1)} %up_hbm.1, ...), custom_call_target="tpu_custom_call" | custom-call | flops 12000000000 | bytes 12000000 | tf_op jit(solution)/shard_map/pallas_call | solution.py:611
  167.4 2.2 %copy.12 = bf16[1,2,2,32,3584]{4,3,2,1,0:T(8,128)(2,1)} copy(bf16[1,2,2,32,3584]{4,3,2,1,0:T(8,128)(2,1)} %get-tuple-element.4) | data formatting | bytes 1835008
  169.6 1.3 copy.13

commit v3 on v2

--- a/solution.py
+++ b/solution.py
@@ -292,27 +292,24 @@
             else:
                 mix_b[u, (h - 2) * 64 : (h - 1) * 64] = both
 
-    def hidden(u):
-        first = gath[u, :, 0:HALF]
-        left = dot(first, up[0:HALF]).reshape(16, 2, 8, 512)
-        right = dot(first, up[HALF:]).reshape(16, 2, 8, 512)
-        pre_a = (left[:, 0] + right[:, 1]).reshape(128, 512)
-        last = gath[u, :, HALF:]
-        upper = lax.broadcasted_iota(jnp.int32, (16, 8, 512), 1) < 4
+    def hidden(u, side):
+        rows = slice(side * ROWS, side * ROWS + ROWS)
+        first = gath[u, rows, 0:HALF]
+        left = dot(first, up[0:HALF]).reshape(8, 2, 8, 512)
+        right = dot(first, up[HALF:]).reshape(8, 2, 8, 512)
+        pre_a = (left[:, 0] + right[:, 1]).reshape(64, 512)
+        last = gath[u, rows, HALF:]
+        upper = lax.broadcasted_iota(jnp.int32, (8, 8, 512), 1) < 4
         quart = [
-            dot(last, up[g * QUART : (g + 1) * QUART]).reshape(16, 2, 8, 512)[:, g // 2]
+            dot(last, up[g * QUART : (g + 1) * QUART]).reshape(8, 2, 8, 512)[:, g // 2]
             for g in range(4)
         ]
         halves = jnp.where(upper, quart[0] + quart[2], quart[1] + quart[3])
-        pre_b = (halves + pltpu.roll(halves, 4, 1)).reshape(128, 512)
-        act_a = (pre_a * jax.nn.sigmoid(pre_a)).astype(BF16)
-        act_b = (pre_b * jax.nn.sigmoid(pre_b)).astype(BF16)
-        return act_a, act_b
-
-    def project(u, act_a, act_b, side):
-        acts = jnp.concatenate(
-            [act_a[side * 64 : side * 64 + 64], act_b[side * 64 : side * 64 + 64]], axis=0
-        )
+        pre_b = (halves + pltpu.roll(halves, 4, 1)).reshape(64, 512)
+        pre = jnp.concatenate([pre_a, pre_b], axis=0)
+        return (pre * jax.nn.sigmoid(pre)).astype(BF16)
+
+    def project(u, acts, side):
         left = dot(acts, down[:, 0:HALF])
         right = dot(acts, down[:, HALF:])
         rows = slice(side * ROWS, side * ROWS + ROWS)
@@ -331,23 +328,13 @@
         )
         part[u, rows, HALF:] = last.reshape(ROWS, QUART).astype(BF16)
 
-    def compute(u, between=()):
-        between = list(between)
-
-        def run(count):
-            for _ in range(min(count, len(between))):
-                between.pop(0)()
-
+    def compute_own(u):
+        project(u, hidden(u, 0), 0)
+
+    def compute_other(u):
         for i in range(8):
             y_copy(u, i).wait_recv()
-        act_a, act_b = hidden(u)
-        run(3)
-        project(u, act_a, act_b, 1)
-        for i in range(8):
-            s_copy(u, i).start()
-        run(2)
-        project(u, act_a, act_b, 0)
-        run(len(between))
+        project(u, hidden(u, 1), 1)
 
     def give_back(u, i):
         s_copy(u, i).wait_recv()
@@ -434,156 +421,168 @@
     norm(0)
     pack(0)
     pl.semaphore_wait(barrier, 8 + (sec > 0).astype(jnp.int32) + (sec < sections - 1).astype(jnp.int32))
+    z_copy(0, 1).start()
     z_copy(0, 0).start()
-    z_copy(0, 1).start()
-    z_copy(0, 2).start()
-    z_copy(0, 3).start()
-    z_copy(0, 4).start()
-    z_copy(0, 5).start()
-    z_copy(0, 6).start()
     y_copy(0, 7).start()
     gath[0, block(me)] = packed[0, block(me)]
+    loads[2].wait()
+    loads[3].wait()
+    z_copy(0, 4).start()
+    z_copy(0, 2).start()
     slots(1)
+    z_copy(0, 5).start()
+    forward(0, 1)
+    z_copy(0, 3).start()
+    z_copy(0, 6).start()
     loads[1].wait()
     norm(1)
     pack(1)
-    z_copy(1, 0).start()
     z_copy(1, 1).start()
-    z_copy(1, 2).start()
-    z_copy(1, 3).start()
-    z_copy(1, 4).start()
-    z_copy(1, 5).start()
-    z_copy(1, 6).start()
+    forward(0, 0)
     y_copy(1, 7).start()
     gath[1, block(me)] = packed[1, block(me)]
-    gate(0)
-    gate(1)
-    forward(0, 0)
-    forward(0, 1)
+    forward(0, 4)
+    z_copy(1, 0).start()
+    forward(0, 5)
     forward(0, 2)
+    z_copy(1, 4).start()
     forward(0, 3)
-    forward(0, 4)
-    forward(0, 5)
+    z_copy(1, 5).start()
     forward(0, 6)
-    loads[2].wait()
-    loads[3].wait()
-    slots(2)
-    slots(3)
+    forward(1, 1)
+    z_copy(1, 6).start()
+    z_copy(1, 2).start()
     forward(1, 0)
-    forward(1, 1)
-    for i in range(8):
-        y_copy(0, i).wait_recv()
-    hid0 = hidden(0)
-    project(0, *hid0, 1)
-    for i in range(8):
-        s_copy(0, i).start()
-    forward(1, 2)
-    forward(1, 3)
-    project(0, *hid0, 0)
-    forward(1, 4)
-    give_back(0, 0)
+    compute_own(0)
+    compute_other(0)
+    s_copy(0, 4).start()
+    s_copy(0, 1).start()
+    z_copy(1, 3).start()
+    s_copy(0, 2).start()
+    s_copy(0, 0).start()
     forward(1, 5)
-    give_back(0, 1)
     forward(1, 6)
     give_back(0, 2)
+    forward(1, 4)
+    forward(1, 3)
+    give_back(0, 1)
+    forward(1, 2)
+    give_back(0, 4)
+    give_back(0, 0)
+    s_copy(0, 5).start()
+    s_copy(0, 6).start()
+    compute_own(1)
+    s_copy(0, 3).start()
+    give_back(0, 5)
+    compute_other(1)
+    s_copy(1, 0).start()
+    give_back(0, 6)
     give_back(0, 3)
-    for i in range(8):
-        y_copy(1, i).wait_recv()
-    hid1 = hidden(1)
-    project(1, *hid1, 1)
-    for i in range(8):
-        s_copy(1, i).start()
-    give_back(0, 4)
-    give_back(0, 5)
-    project(1, *hid1, 0)
-    give_back(0, 6)
+    s_copy(0, 7).start()
+    s_copy(1, 4).start()
+    slots(2)
+    s_copy(1, 1).start()
+    give_back(1, 0)
+    s_copy(1, 2).start()
+    gate(0)
+    s_copy(1, 3).start()
+    s_copy(1, 5).start()
+    gate(1)
+    give_back(1, 4)
     give_back(0, 7)
-    give_back(1, 0)
     give_back(1, 1)
+    s_copy(1, 6).start()
     combine(0)
     shift(0)
     give_back(1, 2)
     give_back(1, 3)
+    give_back(1, 5)
     arrive(0)
     norm(2)
     pack(2)
+    z_copy(2, 1).start()
+    s_copy(1, 7).start()
+    z_copy(2, 2).start()
+    give_back(1, 6)
+    z_copy(2, 3).start()
+    give_back(1, 7)
+    forward(2, 1)
     z_copy(2, 0).start()
-    z_copy(2, 1).start()
-    z_copy(2, 2).start()
-    z_copy(2, 3).start()
     z_copy(2, 4).start()
     z_copy(2, 5).start()
-    z_copy(2, 6).start()
     y_copy(2, 7).start()
     gath[2, block(me)] = packed[2, block(me)]
-    gate(2)
-    give_back(1, 4)
-    forward(2, 0)
-    give_back(1, 5)
-    forward(2, 1)
-    give_back(1, 6)
-    forward(2, 2)
-    give_back(1, 7)
-    forward(2, 3)
     combine(1)
     shift(1)
-    forward(2, 4)
+    forward(2, 2)
+    forward(2, 3)
+    slots(3)
+    z_copy(2, 6).start()
+    forward(2, 0)
     arrive(1)
     norm(3)
     pack(3)
     z_copy(3, 0).start()
     z_copy(3, 1).start()
-    z_copy(3, 2).start()
-    z_copy(3, 3).start()
-    z_copy(3, 4).start()
-    z_copy(3, 5).start()
-    z_copy(3, 6).start()
     y_copy(3, 7).start()
     gath[3, block(me)] = packed[3, block(me)]
+    z_copy(3, 3).start()
     forward(2, 5)
+    forward(2, 4)
+    gate(3)
+    gate(2)
+    z_copy(3, 6).start()
+    forward(3, 1)
     forward(2, 6)
-    gate(3)
+    compute_own(2)
+    forward(3, 0)
+    z_copy(3, 4).start()
+    forward(3, 3)
+    compute_other(2)
+    s_copy(2, 0).start()
+    z_copy(3, 5).start()
+    z_copy(3, 2).start()
+    s_copy(2, 2).start()
     grad_local()
+    forward(3, 6)
+    s_copy(2, 1).start()
+    give_back(2, 0)
+    s_copy(2, 4).start()
     grad_share()
-    forward(3, 0)
-    forward(3, 1)
-    for i in range(8):
-        y_copy(2, i).wait_recv()
-    hid2 = hidden(2)
-    project(2, *hid2, 1)
-    for i in range(8):
-        s_copy(2, i).start()
-    forward(3, 2)
-    forward(3, 3)
-    project(2, *hid2, 0)
+    give_back(2, 2)
     forward(3, 4)
-    give_back(2, 0)
+    give_back(2, 4)
     forward(3, 5)
     give_back(2, 1)
-    forward(3, 6)
-    give_back(2, 2)
+    forward(3, 2)
+    compute_own(3)
+    s_copy(2, 3).start()
+    s_copy(2, 6).start()
+    compute_other(3)
+    s_copy(3, 0).start()
+    s_copy(3, 1).start()
+    s_copy(2, 5).start()
     give_back(2, 3)
-    for i in range(8):
-        y_copy(3, i).wait_recv()
-    hid3 = hidden(3)
-    project(3, *hid3, 1)
-    for i in range(8):
-        s_copy(3, i).start()
-    give_back(2, 4)
-    give_back(2, 5)
-    project(3, *hid3, 0)
-    give_back(2, 6)
-    give_back(2, 7)
+    s_copy(3, 4).start()
+    s_copy(3, 3).start()
     give_back(3, 0)
     give_back(3, 1)
+    s_copy(3, 2).start()
+    s_copy(3, 6).start()
+    give_back(2, 6)
+    s_copy(3, 5).start()
+    give_back(3, 4)
+    give_back(3, 3)
+    give_back(3, 2)
+    s_copy(2, 7).start()
+    give_back(3, 6)
+    give_back(2, 5)
+    give_back(3, 5)
+    s_copy(3, 7).start()
+    grad_total()
+    give_back(2, 7)
     combine(2)
-    give_back(3, 2)
-    give_back(3, 3)
-    give_back(3, 4)
-    give_back(3, 5)
-    give_back(3, 6)
     give_back(3, 7)
-    grad_total()
     combine(3)
 
     for u in range(UNITS):
@@ -605,6 +604,46 @@
 
 def per_device(held, entering, gain, router, up, down, routes, cot):
     width = up.shape[-1]
+    moved, total = exchange(width, held, entering, gain, router, up, down, routes, cot)
+    hbm = pl.BlockSpec(memory_space=pl.ANY)
+    return pl.pallas_call(
+        settle,
+        out_shape=(
+            jax.ShapeDtypeStruct(moved.shape, moved.dtype),
+            jax.ShapeDtypeStruct(total.shape, total.dtype),
+        ),
+        in_specs=[hbm, hbm],
+        out_specs=(hbm, hbm),
+        scratch_shapes=[
+            pltpu.VMEM(moved.shape, moved.dtype),
+            pltpu.VMEM(total.shape, total.dtype),
+            pltpu.SemaphoreType.DMA((UNITS + 1,)),
+            pltpu.SemaphoreType.DMA((UNITS + 1,)),
+        ],
+    )(moved, total)
+
+
+def settle(moved, total, layer_out, grads, rows, sums, fetch, store):
+    pieces = [(moved, rows, layer_out, (0, u // 2, u % 2)) for u in range(UNITS)]
+    pieces.append((total, sums, grads, (0,)))
+    reads = [
+        pltpu.make_async_copy(source.at[at], held.at[at], fetch.at[i])
+        for i, (source, held, _, at) in enumerate(pieces)
+    ]
+    writes = [
+        pltpu.make_async_copy(held.at[at], dest.at[at], store.at[i])
+        for i, (_, held, dest, at) in enumerate(pieces)
+    ]
+    for read in reads:
+        read.start()
+    for read, write in zip(reads, writes):
+        read.wait()
+        write.start()
+    for write in writes:
+        write.wait()
+
+
+def exchange(width, held, entering, gain, router, up, down, routes, cot):
     hbm = pl.BlockSpec(memory_space=pl.ANY)
     vmem = pl.BlockSpec(memory_space=pltpu.VMEM)
     dma = pltpu.SemaphoreType.DMA

time: 173 us -> 154 us (0.89)
  Pallas kernels: 167 us -> 151 us
  local copies, waits for them, and re-layouts: 3.46 us -> 0 us
    pallas_call x1 -> x2, Pallas kernels: 167 us -> 151 us  [the longest x1 149 us: exchange(): pl.pallas_call(kernel, out_shape=(jax.ShapeDtypeStruct((1, TICKS, 2, TOK,...]
    unnamed x2 -> x0, local copies, waits for them, and re-layouts: 3.46 us -> none
where the time goes in v3:
time: 154 us; the launch traced here: 152 us
  Pallas kernels  151 us (98%)
    pallas_call x1, Pallas kernels, exchange(): pl.pallas_call(kernel, out_shape=(jax.ShapeDtypeStruct((1, TICKS, 2, TOK,...  149 us

profile of v3, /device:TPU:15, one launch (start us, length us, event | category | flops | bytes accessed | tf_op | source)
XLA Modules:
  0.0 151.7 jit_solution(17212084282420188305)
XLA Ops:
  0.6 148.8 %shard_map.95 = (bf16[1,2,2,32,3584]{4,3,2,1,0:T(8,128)(2,1)}, f32[1,8,224]{2,1,0:T(8,128)}) custom-call(bf16[1,2,32,3584]{3,2,1,0:T(8,128)(2,1)} %held.1, bf16[1,2,32,3584]{3,2,1,0:T(8,128)(2,1)} %entering.1, bf16[1,3584]{1,0:T(2,128)(2,1)} %gain.1, bf16[1,8,3584]{2,1,0:T(8,128)(2,1)} %router.1, bf16[1,1,3584,512]{3,2,1,0:T(8,128)(2,1)} %up_hbm.1, ...), custom_call_target="tpu_custom_call" | custom-call | flops 12000000000 | bytes 12000000 | tf_op jit(solution)/shard_map/pallas_call | solution.py:650
  149.5 2.1 %shard_map.96 = (bf16[1,2,2,32,3584]{4,3,2,1,0:T(8,128)(2,1)}, f32[1,8,224]{2,1,0:T(8,128)}) custom-call(bf16[1,2,2,32,3584]{4,3,2,1,0:T(8,128)(2,1)} %get-tuple-element.4.moved, f32[1,8,224]{2,1,0:T(8,128)} %get-tuple-element.5.total), custom_call_target="tpu_custom_call" | custom-call | tf_op jit(solution)/shard_map/pallas_call | solution.py:609

commit v4 on v3

--- a/solution.py
+++ b/solution.py
@@ -117,8 +117,8 @@
         pltpu.make_async_copy(up_hbm.at[0, 0], up, in_sem.at[2]),
         pltpu.make_async_copy(down_hbm.at[0, 0], down, in_sem.at[3]),
     ]
-    for load in loads:
-        load.start()
+    loads[0].start()
+    loads[1].start()
     enter_up = pltpu.make_async_copy(entering.at[0, 0], states.at[2], in_sem.at[4])
     enter_down = pltpu.make_async_copy(entering.at[0, 1], states.at[3], in_sem.at[5])
 
@@ -418,6 +418,8 @@
     turn()
     slots(0)
     loads[0].wait()
+    loads[2].start()
+    loads[3].start()
     norm(0)
     pack(0)
     pl.semaphore_wait(barrier, 8 + (sec > 0).astype(jnp.int32) + (sec < sections - 1).astype(jnp.int32))

time: 154 us -> 153 us (level)
  no operation moved by 1% of the time
where the time goes in v4:
time: 153 us; the launch traced here: 151 us
  Pallas kernels  150 us (98%)
    pallas_call x1, Pallas kernels, exchange(): pl.pallas_call(kernel, out_shape=(jax.ShapeDtypeStruct((1, TICKS, 2, TOK,...  148 us

profile of v4, /device:TPU:15, one launch (start us, length us, event | category | flops | bytes accessed | tf_op | source)
XLA Modules:
  0.0 150.9 jit_solution(8342938038646957611)
XLA Ops:
  0.6 148.1 %shard_map.95 = (bf16[1,2,2,32,3584]{4,3,2,1,0:T(8,128)(2,1)}, f32[1,8,224]{2,1,0:T(8,128)}) custom-call(bf16[1,2,32,3584]{3,2,1,0:T(8,128)(2,1)} %held.1, bf16[1,2,32,3584]{3,2,1,0:T(8,128)(2,1)} %entering.1, bf16[1,3584]{1,0:T(2,128)(2,1)} %gain.1, bf16[1,8,3584]{2,1,0:T(8,128)(2,1)} %router.1, bf16[1,1,3584,512]{3,2,1,0:T(8,128)(2,1)} %up_hbm.1, ...), custom_call_target="tpu_custom_call" | custom-call | flops 12000000000 | bytes 12000000 | tf_op jit(solution)/shard_map/pallas_call | solution.py:652
  148.7 2.1 %shard_map.96 = (bf16[1,2,2,32,3584]{4,3,2,1,0:T(8,128)(2,1)}, f32[1,8,224]{2,1,0:T(8,128)}) custom-call(bf16[1,2,2,32,3584]{4,3,2,1,0:T(8,128)(2,1)} %get-tuple-element.4.moved, f32[1,8,224]{2,1,0:T(8,128)} %get-tuple-element.5.total), custom_call_target="tpu_custom_call" | custom-call | tf_op jit(solution)/shard_map/pallas_call | solution.py:611
